TPU v7x, 512 devices: a whole 4x8x8 slice. The times are simulated.
512 devices in a mesh: tm: 64 (over y, x, core), head: 8 (over z).
Axes of the slice: x: 4, y: 8, z: 8, core: 2. Of those that a mesh axis runs over, the one named last changes fastest.
Arguments:
- queries: bfloat16 [8192, 1024], P('tm', 'head'), may hold values from -5.2 to 5.2
- keys: bfloat16 [8192, 1024], P('tm', 'head'), may hold values from -5.2 to 5.2
- values: bfloat16 [8192, 1024], P('tm', 'head'), may hold values from -24 to 24
- out_weight: bfloat16 [5120, 1024], P(None, 'head'), may hold values from -0.1875 to 0.1875
- output_cotangent: bfloat16 [8192, 5120], P('tm'), may hold values from -6 to 6
- block_mask: int32 [64, 64], replicated, may hold values from 0 to 1, as said below
- segment_of_device: int32 [64], replicated, may hold values from 0 to 63, each once
Outputs:
- layer_output: bfloat16 [8192, 5120], P('tm', 'head')
- query_grad: bfloat16 [8192, 1024], P('tm', 'head')
- key_grad: bfloat16 [8192, 1024], P('tm', 'head')
- value_grad: bfloat16 [8192, 1024], P('tm', 'head')
Inputs may be any that keep to these rules, and one draw needn't show every extreme that they name: block_mask[i, j] = 1 lets the queries of sequence block i (128 tokens) see the keys of block j; two blocks of one latent frame (1024 tokens) always see each other; for frames further apart each query block sees a band of key blocks of the other frame whose width halves with the distance level, at least one block. Rows i * 128 to (i + 1) * 128 - 1 of every token-indexed array hold the sequence's segment segment_of_device[i] of 128 tokens; each segment appears once.
All inputs are finite; a program needn't handle non-finite values.
Results may differ from a plain program's by a relative error of at most 0.04.
Values may be sent and summed in bfloat16 or wider, within the bound.
A program may use at most 64 MiB of HBM per device.

v0:
```python
import math

import jax
import jax.numpy as jnp
from jax import lax
from jax.sharding import PartitionSpec as P

HD = 128
BLK = 128


MASKED_SCORE = -1e30


def block_ids(segment_of_device, first_row, row_count, per_device):
    row_index = first_row + jnp.arange(row_count, dtype=jnp.int32)
    owner_device = row_index // per_device
    device_table = jnp.arange(segment_of_device.shape[0], dtype=jnp.int32)
    picked = jnp.where(
        owner_device[:, None] == device_table[None, :], segment_of_device[None, :], 0
    )
    segment = jnp.sum(picked, axis=1)
    return (segment * per_device + row_index % per_device) // BLK


def one_hot(block_index, total_blocks):
    return (block_index[:, None] == jnp.arange(total_blocks, dtype=jnp.int32)[None, :]).astype(
        jnp.float32
    )


def pair_scores(left, right):
    return lax.dot_general(
        left, right, (((1,), (1,)), ((), ())), preferred_element_type=jnp.float32
    )


def row_products(left, right):
    return lax.dot_general(
        left, right, (((0,), (0,)), ((), ())), preferred_element_type=jnp.float32
    )


def local(queries, keys, values, out_weight, output_cotangent, block_mask, segment_of_device):
    per_device = queries.shape[0]
    total_blocks = block_mask.shape[0]
    score_scale = 1.0 / math.sqrt(HD)
    mask_float = block_mask.astype(jnp.float32)
    own_first = lax.axis_index("tm") * per_device
    own_hot = one_hot(block_ids(segment_of_device, own_first, per_device, per_device), total_blocks)
    row_links = jnp.dot(own_hot, mask_float)
    column_links = jnp.dot(mask_float, own_hot.T)

    def key_links(first_row, row_count):
        piece_hot = one_hot(
            block_ids(segment_of_device, first_row, row_count, per_device), total_blocks
        )
        return jnp.dot(row_links, piece_hot.T) > 0.5

    def masked_scores(linked, key_piece):
        return jnp.where(linked, pair_scores(queries, key_piece) * score_scale, MASKED_SCORE)

    start_max = jnp.full((per_device,), MASKED_SCORE, jnp.float32)
    key_piece = lax.all_gather(keys, "tm", axis=0, tiled=True)
    linked = key_links(jnp.int32(0), key_piece.shape[0])
    scores = masked_scores(linked, key_piece)
    new_max = jnp.maximum(start_max, jnp.max(scores, axis=1))
    weights = jnp.where(linked, jnp.exp(scores - new_max[:, None]), 0.0)
    row_sum = jnp.sum(weights, axis=1)
    row_lse = new_max + jnp.log(row_sum)
    key_piece = lax.all_gather(keys, "tm", axis=0, tiled=True)
    value_piece = lax.all_gather(values, "tm", axis=0, tiled=True)
    linked = key_links(jnp.int32(0), key_piece.shape[0])
    scores = masked_scores(linked, key_piece)
    weights = jnp.exp(scores - row_lse[:, None]).astype(jnp.bfloat16)
    attended_sum = jnp.dot(weights, value_piece, preferred_element_type=jnp.float32)
    attended = attended_sum.astype(jnp.bfloat16)
    summed = lax.psum_scatter(
        pair_scores(out_weight, attended).astype(jnp.bfloat16),
        "head",
        scatter_dimension=0,
        tiled=True,
    ).astype(jnp.float32)
    layer_output = summed.T.astype(jnp.bfloat16)
    out_grad = jnp.dot(output_cotangent, out_weight, preferred_element_type=jnp.float32).astype(
        jnp.bfloat16
    )
    row_delta = jnp.sum(out_grad.astype(jnp.float32) * attended.astype(jnp.float32), axis=1)
    key_piece = lax.all_gather(keys, "tm", axis=0, tiled=True)
    value_piece = lax.all_gather(values, "tm", axis=0, tiled=True)
    linked = key_links(jnp.int32(0), key_piece.shape[0])
    scores = masked_scores(linked, key_piece)
    exact_probs = jnp.exp(scores - row_lse[:, None])
    slopes = pair_scores(out_grad, value_piece)
    score_grad = (exact_probs * (slopes - row_delta[:, None])).astype(jnp.bfloat16)
    query_total = jnp.dot(score_grad, key_piece, preferred_element_type=jnp.float32)
    query_grad = (query_total * score_scale).astype(jnp.bfloat16)
    query_piece = lax.all_gather(queries.astype(jnp.float32), "tm", axis=0, tiled=True).astype(
        jnp.bfloat16
    )
    grad_piece = lax.all_gather(out_grad.astype(jnp.float32), "tm", axis=0, tiled=True).astype(
        jnp.bfloat16
    )
    lse_piece = lax.all_gather(row_lse, "tm", axis=0, tiled=True)
    delta_piece = lax.all_gather(row_delta, "tm", axis=0, tiled=True)
    piece_hot = one_hot(
        block_ids(segment_of_device, jnp.int32(0), query_piece.shape[0], per_device), total_blocks
    )
    linked = jnp.dot(piece_hot, column_links) > 0.5
    scores = jnp.where(linked, pair_scores(query_piece, keys) * score_scale, MASKED_SCORE)
    exact_probs = jnp.exp(scores - lse_piece[:, None])
    slopes = pair_scores(grad_piece, values)
    score_grad = (exact_probs * (slopes - delta_piece[:, None])).astype(jnp.bfloat16)
    weights = exact_probs.astype(jnp.bfloat16)
    key_total = row_products(score_grad, query_piece)
    value_total = row_products(weights, grad_piece)
    key_total, value_total = (key_total, value_total)
    key_grad = (key_total * score_scale).astype(jnp.bfloat16)
    value_grad = value_total.astype(jnp.bfloat16)
    return (layer_output, query_grad, key_grad, value_grad)


def solution(mesh):
    return jax.shard_map(
        local,
        mesh=mesh,
        in_specs=(
            P("tm", "head"),
            P("tm", "head"),
            P("tm", "head"),
            P(None, "head"),
            P("tm", None),
            P(),
            P(),
        ),
        out_specs=(P("tm", "head"), P("tm", "head"), P("tm", "head"), P("tm", "head")),
        check_vma=False,
    )
```

profile of v0, /device:TPU:1, one launch (start us, length us, event | category | flops | bytes accessed | tf_op | source)
XLA Modules:
  0.0 395.5 jit_solution(5750930479014700791)
XLA Ops:
  7.2 0.0 all-gather.7.cloned.1.call-start
  7.2 0.7 all-gather.7.cloned.1.call-update
  7.9 0.0 all-gather.9.cloned.1.call-start
  8.0 0.7 all-gather.9.cloned.1.call-update
  8.7 0.0 all-gather.11.cloned.1.call-start
  8.7 0.7 all-gather.11.cloned.1.call-update
  9.4 0.0 all-gather.13.cloned.1.call-start
  9.5 2.6 convolution_convert_fusion.1
  12.0 0.0 all-gather.13.cloned.1.call-update
  12.1 0.0 reduce-scatter.4.cloned.1.call-start
  12.2 0.1 select_reduce_fusion.2
  12.2 0.4 select_reduce_fusion.1
  12.7 1.2 convolution_compare_fusion.1
  14.0 85.8 %all-gather.7.cloned.1.call-done = bf16[8192,128]{1,0:T(8,128)(2,1)} async-done(((bf16[128,128]{1,0:T(8,128)(2,1)}), bf16[8192,128]{1,0:T(8,128)(2,1)}) %all-gather.7.cloned.1.call-update) | async-done | bytes 2097168 | tf_op jit(solution)/shard_map/all_gather | solution.py:71
  99.8 2.6 fusion.57
  102.4 1.2 select_reduce_fusion
  103.6 0.7 copy-done.1
  104.3 79.4 %all-gather.9.cloned.1.call-done = bf16[8192,128]{1,0:T(8,128)(2,1)} async-done(((bf16[128,128]{1,0:T(8,128)(2,1)}), bf16[8192,128]{1,0:T(8,128)(2,1)}) %all-gather.9.cloned.1.call-update) | async-done | bytes 2097168 | tf_op jit(solution)/shard_map/all_gather | solution.py:72
  183.7 4.0 %multiply_reduce_fusion = (f32[128]{0:T(128)S(1)}, bf16[128,128]{0,1:T(8,128)(2,1)S(1)}) fusion(bf16[128,128]{0,1:T(8,128)(2,1)S(1)} %copy-done.3, bf16[8192,128]{1,0:T(8,128)(2,1)} %all-gather.9.cloned.1.call-done, f32[128,8192]{1,0:T(8,128)} %copy-done.1, f32[128]{0:T(128)S(1)} %log_add_fusion), kind=kOutput, calls=%fused_computation.43 | convolution fusion | flops 270614400 | bytes 6358016 | tf_op jit(solution)/shard_map/dot_general | solution.py:76
  187.7 0.5 fusion.8
  188.2 1.4 copy.11
  189.7 1.4 convolution_compare_fusion
  191.1 33.9 %all-gather = f32[64,1,128]{2,1,0:T(1,128)S(1)} all-gather(f32[1,1,128]{2,1,0:T(1,128)S(1)} %bitcast.27), channel_id=1, replica_groups=mesh['tm'=64,'head'=8] {'tm'}, dimensions={0}, use_global_device_ids=true | all-gather | bytes 33280 | tf_op jit(solution)/shard_map/all_gather | solution.py:104
  225.0 34.1 %all-gather.1 = f32[64,1,128]{2,1,0:T(1,128)S(1)} all-gather(f32[1,1,128]{2,1,0:T(1,128)S(1)} %bitcast.28), channel_id=1, replica_groups=mesh['tm'=64,'head'=8] {'tm'}, dimensions={0}, use_global_device_ids=true | all-gather | bytes 33280 | tf_op jit(solution)/shard_map/all_gather | solution.py:105
  259.1 8.5 %all-gather.11.cloned.1.call-done = bf16[8192,128]{1,0:T(8,128)(2,1)} async-done(((bf16[128,128]{1,0:T(8,128)(2,1)}), bf16[8192,128]{1,0:T(8,128)(2,1)}) %all-gather.11.cloned.1.call-update) | async-done | bytes 2097168 | tf_op jit(solution)/shard_map/all_gather | solution.py:98
  267.6 4.0 %fusion.3 = f32[8192,128]{1,0:T(8,128)} fusion(pred[8192,128]{1,0:T(32,128)(4,1)S(1)} %convolution_compare_fusion, bf16[128,128]{1,0:T(8,128)(2,1)S(1)} %copy-done.5, f32[8192]{0:T(1024)S(1)} %bitcast.24, bf16[8192,128]{1,0:T(8,128)(2,1)} %all-gather.11.cloned.1.call-done), kind=kOutput, calls=%fused_computation.5 | convolution fusion | flops 271581184 | bytes 7405568 | tf_op jit(solution)/shard_map/dot_general | solution.py:33
  271.6 75.4 %all-gather.13.cloned.1.call-done = bf16[8192,128]{0,1:T(8,128)(2,1)} async-done(((bf16[128,128]{0,1:T(8,128)(2,1)}), bf16[8192,128]{0,1:T(8,128)(2,1)}) %all-gather.13.cloned.1.call-update) | async-done | bytes 2097168 | tf_op jit(solution)/shard_map/all_gather | solution.py:101
  347.0 4.2 %fusion.24 = bf16[128,128]{1,0:T(8,128)(2,1)} fusion(f32[8192,128]{1,0:T(8,128)} %fusion.3, bf16[8192,128]{0,1:T(8,128)(2,1)} %all-gather.13.cloned.1.call-done), kind=kOutput, calls=%fused_computation.33 | convolution fusion | flops 269500416 | bytes 6324224 | tf_op jit(solution)/shard_map/dot_general | solution.py:39
  351.2 6.4 %fusion.19 = bf16[128,128]{1,0:T(8,128)(2,1)} fusion(f32[8192,128]{1,0:T(8,128)} %fusion.3, bf16[128,128]{1,0:T(8,128)(2,1)S(1)} %copy-done.6, f32[8192]{0:T(1024)S(1)} %bitcast.26, bf16[8192,128]{0,1:T(8,128)(2,1)} %all-gather.13.cloned.1.call-done, bf16[8192,128]{1,0:T(8,128)(2,1)S(1)} %copy-done.2), kind=kOutput, calls=%fused_computation.30 | convolution fusion | flops 540049408 | bytes 8486912 | tf_op jit(solution)/shard_map/dot_general | solution.py:39
  357.6 5.7 %fusion.20 = bf16[128,128]{1,0:T(8,128)(2,1)} fusion(bf16[8192,128]{1,0:T(8,128)(2,1)} %all-gather.7.cloned.1.call-done, bf16[128,128]{0,1:T(8,128)(2,1)S(1)} %copy-done.3, bf16[8192,128]{1,0:T(8,128)(2,1)} %all-gather.9.cloned.1.call-done, f32[128,8192]{1,0:T(8,128)} %copy-done.1, f32[128]{0:T(128)S(1)} %get-tuple-element.6, f32[128]{0:T(128)S(1)} %log_add_fusion), kind=kOutput, calls=%fused_computation.31 | convolution fusion | flops 541097984 | bytes 8455168 | tf_op jit(solution)/shard_map/dot_general | solution.py:96
  363.3 24.0 %reduce-scatter.4.cloned.1.call-done = bf16[640,128]{1,0:T(8,128)(2,1)} async-done(((bf16[5120,128]{1,0:T(8,128)(2,1)}), bf16[640,128]{1,0:T(8,128)(2,1)}) %reduce-scatter.4.cloned.1.call-update) | async-done | bytes 163856
  387.2 1.7 copy.12
  (24 shorter events, 0.1 us)
Async XLA Ops:
  7.2 2.3 copy-start
  7.2 5.0 %copy-start.7 = (s32[64]{0:T(128)S(1)}, s32[64]{0:T(128)}, u32[]{:S(2)}) copy-start(s32[64]{0:T(128)} %param.13) | copy-start | bytes 772
  7.2 5.5 %copy-start.8 = (s32[64,64]{1,0:T(8,128)S(1)}, s32[64,64]{1,0:T(8,128)}, u32[]{:S(2)}) copy-start(s32[64,64]{1,0:T(8,128)} %param.12) | copy-start | bytes 49156
  7.2 92.6 %all-gather.7.cloned.1.call-start = ((), (), s32[]{:S(2)}) async-start(), calls=%async_computation.1 | async-start | bytes 2129920 | tf_op jit(solution)/shard_map/all_gather | solution.py:71
  7.9 175.7 %all-gather.9.cloned.1.call-start = ((), (), s32[]{:S(2)}) async-start(), calls=%async_computation.2 | async-start | bytes 2129920 | tf_op jit(solution)/shard_map/all_gather | solution.py:72
  8.7 258.9 %all-gather.11.cloned.1.call-start = ((), (), s32[]{:S(2)}) async-start(), calls=%async_computation.3 | async-start | bytes 2129920 | tf_op jit(solution)/shard_map/all_gather | solution.py:98
  9.4 337.6 %all-gather.13.cloned.1.call-start = ((), (), s32[]{:S(2)}) async-start(), calls=%async_computation.4 | async-start | bytes 2129920 | tf_op jit(solution)/shard_map/all_gather | solution.py:101
  12.1 375.2 %reduce-scatter.4.cloned.1.call-start = ((), (), s32[]{:S(2)}) async-start(), calls=%async_computation.5 | async-start | bytes 1474560
  12.7 87.1 %copy-start.4 = (bf16[128,128]{1,0:T(8,128)(2,1)S(1)}, bf16[128,128]{1,0:T(8,128)(2,1)}, u32[]{:S(2)}) copy-start(bf16[128,128]{1,0:T(8,128)(2,1)} %param.7) | copy-start | bytes 98308
  102.4 1.9 copy-start.1
  102.4 81.3 %copy-start.3 = (bf16[128,128]{0,1:T(8,128)(2,1)S(1)}, bf16[128,128]{0,1:T(8,128)(2,1)}, u32[]{:S(2)}) copy-start(bf16[128,128]{0,1:T(8,128)(2,1)} %convolution_convert_fusion.1) | copy-start | bytes 98308
  189.7 77.9 %copy-start.5 = (bf16[128,128]{1,0:T(8,128)(2,1)S(1)}, bf16[128,128]{1,0:T(8,128)(2,1)}, u32[]{:S(2)}) copy-start(bf16[128,128]{1,0:T(8,128)(2,1)} %param.8) | copy-start | bytes 98308
  271.6 79.6 %copy-start.2 = (bf16[8192,128]{1,0:T(8,128)(2,1)S(1)}, bf16[8192,128]{1,0:T(8,128)(2,1)}, u32[]{:S(2)}) copy-start(bf16[8192,128]{1,0:T(8,128)(2,1)} %all-gather.11.cloned.1.call-done) | copy-start | bytes 6291460
  271.6 79.6 %copy-start.6 = (bf16[128,128]{1,0:T(8,128)(2,1)S(1)}, bf16[128,128]{1,0:T(8,128)(2,1)}, u32[]{:S(2)}) copy-start(bf16[128,128]{1,0:T(8,128)(2,1)} %param.9) | copy-start | bytes 98308
Sparse Core Ops, SparseCore 0:
  11.4 88.3 all-gather.6
  103.1 80.5 all-gather.8
  187.0 80.5 all-gather.10
  271.3 75.6 all-gather.12
  349.7 37.5 reduce-scatter.3
where the time goes:
time: 399 us; the launch traced here: 395 us
  waiting for transfers between devices  275 us (69%)
  blocking collectives  68 us (17%)
  matrix products  32.6 us (8%)
  between operations  13.9 us (3%)
    all_gather x1, waiting for transfers between devices, local(): key_piece = lax.all_gather(keys, 'tm', axis=0, tiled=True)  85.8 us
    all_gather x1, waiting for transfers between devices, local(): value_piece = lax.all_gather(values, 'tm', axis=0, tiled=True)  79.4 us
    all_gather x1, waiting for transfers between devices, local(): lax.all_gather(out_grad.astype(jnp.float32), 'tm', axis=0, tiled=True)  75.4 us
    all_gather x1, blocking collectives, local(): delta_piece = lax.all_gather(row_delta, 'tm', axis=0, tiled=True)  34.1 us
    all_gather x1, blocking collectives, local(): lse_piece = lax.all_gather(row_lse, 'tm', axis=0, tiled=True)  33.9 us
    unnamed x6, waiting for transfers between devices  26 us
    dot_general x2, matrix products, row_products(): lax.dot_general(left, right, (((0,), (0,)), ((), ())), preferred_element_...  10.6 us
    all_gather x1, waiting for transfers between devices, local(): lax.all_gather(queries.astype(jnp.float32), 'tm', axis=0, tiled=True)  8.5 us
  transfers between devices with their start and end apart: 5, of which 5 were waited for; matrix products, arithmetic and copies ran while one was open for 9% of the time, Pallas kernels for 0%

commit v1 on v0

v1 whole, which is shorter than its diff:
```python
import functools
import math

import jax
import jax.numpy as jnp
from jax import lax
from jax.experimental import pallas as pl
from jax.experimental.pallas import tpu as pltpu
from jax.sharding import PartitionSpec as P

HD = 128
NX, NY = 4, 8
BLOCKS = 2 * NX * NY
MASKED_SCORE = -1e30
SCALE = 1.0 / math.sqrt(HD)
SCALE2 = SCALE * math.log2(math.e)
MESH = pl.DeviceIdType.MESH
BF, F32 = jnp.bfloat16, jnp.float32

DX = (0, 1, -1, 2)


def nt(left, right):
    return lax.dot_general(left, right, (((1,), (1,)), ((), ())), preferred_element_type=F32)


def nn(left, right):
    return lax.dot_general(left, right, (((1,), (0,)), ((), ())), preferred_element_type=F32)


def kernel(nz, ow, q_hbm, k_hbm, v_hbm, w_hbm, cot_hbm, mask_ref, seg_ref, out_ref, dq_ref, dk_ref, dv_ref,
           ka, vb, qa, ob, s_scr, p_scr, w_own, cot, w_all, att, stat, lsem, ssem, rsem):
    t, z = lax.axis_index("tm"), lax.axis_index("head")
    y, x, c = t // (2 * NX), (t // 2) % NX, t % 2

    def at(dx=0, dy=0, core=0, dz=0):
        col, row = (x + (dx + NX)) % NX, (y + (dy + NY)) % NY
        return ((row * NX + col) * 2 + (c + core) % 2, (z + dz) % nz)

    right, left, across = at(dx=1), at(dx=-1), at(dx=2)
    up, down, sib = at(dy=1), at(dy=-1), at(core=1)

    loads = []

    def load(src, dst):
        cp = pltpu.make_async_copy(src, dst, lsem.at[len(loads)])
        cp.start()
        loads.append(cp)
        return cp

    l_k, l_v, l_q = load(k_hbm, ka.at[0]), load(v_hbm, vb.at[0]), load(q_hbm, qa.at[0])
    l_w, l_c = load(w_hbm, w_own), load(cot_hbm, cot)

    partners = [at(dx=dx, core=cc) for cc in (0, 1) for dx in DX][1:]
    partners += [at(dy=dy) for dy in range(1, NY)] + [at(dz=dz) for dz in range(1, nz)]
    barrier = pltpu.get_barrier_semaphore()
    for who in partners:
        pl.semaphore_signal(barrier, inc=1, device_id=who, device_id_type=MESH)

    l_w.wait()
    l_c.wait()
    grad = nn(cot[...], w_own[...]).astype(BF)
    ob[0] = grad
    l_k.wait()
    l_v.wait()
    l_q.wait()
    pl.semaphore_wait(barrier, len(partners))

    sent = []

    def send(src, dst, who):
        i = len(sent)
        cp = pltpu.make_async_remote_copy(
            src_ref=src, dst_ref=dst, send_sem=ssem.at[i], recv_sem=rsem.at[i], device_id=who, device_id_type=MESH
        )
        cp.start()
        sent.append(cp)
        return cp

    def arrive(*copies):
        for cp in copies:
            cp.wait_recv()

    def rows(buf, i, n):
        return buf.at[pl.ds(i, n)]

    class A:
        def __init__(self, buf):
            self.buf, self.sib = buf, []
            self.line = [send(buf.at[0], buf.at[i], who) for i, who in ((2, right), (1, left), (3, across))]

        def first(self):
            arrive(*self.line)
            b = self.buf
            self.y = [send(rows(b, 0, 4), rows(b, 12, 4), up), send(rows(b, 0, 4), rows(b, 8, 4), down)]

        def wave(self, p):
            arrive(*self.y)
            b, g = self.buf, 8 * p
            if p < 3:
                self.y = [send(rows(b, g + 4, 4), rows(b, g + 12, 4), up), send(rows(b, g, 4), rows(b, g + 8, 4), down)]
            else:
                self.y = [send(rows(b, g + 4, 2), rows(b, 4, 2), up), send(rows(b, g + 2, 2), rows(b, 6, 2), down)]
            self.sib.append(send(rows(b, g, 8), rows(b, 32 + g, 8), sib))

        def last(self):
            arrive(*self.y)
            self.sib.append(send(rows(self.buf, 0, 8), rows(self.buf, 32, 8), sib))

    class B:
        def __init__(self, buf):
            self.buf, self.sib, self.x, self.x2 = buf, [], {}, {}
            b = buf
            self.y = [send(b.at[0], b.at[9], up), send(b.at[0], b.at[8], down)]
            self.x[0] = [send(b.at[0], b.at[4], right), send(b.at[0], b.at[2], left)]

        def wave(self, p):
            arrive(*self.y)
            b, g = self.buf, 8 * p
            if p < 3:
                self.y = [send(b.at[g + 1], b.at[g + 9], up), send(b.at[g], b.at[g + 8], down)]
            elif p == 3:
                top, low = pl.ds(0, 64), pl.ds(64, 64)
                self.y = [send(b.at[g + 1, top], b.at[1, top], up), send(b.at[g, low], b.at[1, low], down)]
            if p < 4:
                self.x[p] = [send(rows(b, g, 2), rows(b, g + 4, 2), right), send(rows(b, g, 2), rows(b, g + 2, 2), left)]
            else:
                self.x[p] = [send(b.at[1], b.at[5], right), send(b.at[1], b.at[3], left)]

        def relay(self, p):
            arrive(*self.x[p])
            b, g = self.buf, 8 * p
            if 1 <= p <= 3:
                self.x2[p] = [send(b.at[g + 4], b.at[g + 6], right), send(b.at[g + 3], b.at[g + 7], left)]
            else:
                k = p // 4
                top, low = pl.ds(0, 64), pl.ds(64, 64)
                self.x2[p] = [
                    send(b.at[4 + k, top], b.at[6 + k, top], right),
                    send(b.at[2 + k, low], b.at[6 + k, low], left),
                ]

        def share(self, p):
            arrive(*self.x2[p])
            if p == 0:
                arrive(*self.x2[4])
            self.sib.append(send(rows(self.buf, 8 * p, 8), rows(self.buf, 32 + 8 * p, 8), sib))

    vals, keys = B(vb), A(ka)
    ques, grads = A(qa), B(ob)
    half = ow // 2
    part = pl.ds(pl.multiple_of(c * half, 16), half)
    w_in = []
    for dz in range(1, nz):
        first = pl.multiple_of(((z + nz - dz) % nz) * ow + c * half, 16)
        w_in.append(send(w_own.at[pl.ds(first, half)], w_all.at[dz, part], at(dz=-dz + nz)))

    own_seg = seg_ref[t]

    def place(g, dxi):
        core, p, k = g // 8, (g // 2) % 4, g % 2
        dy = jnp.where(p == 0, 4 * k, jnp.where(k == 0, p, NY - p))
        col, row = (x + (DX[dxi] + NX)) % NX, (y + dy) % NY
        return seg_ref[(row * NX + col) * 2 + (c + core) % 2]

    def bias_of(link):
        return (1 - link).astype(F32) * MASKED_SCORE

    def chunk_a(buf, g):
        return buf[pl.ds(g * 4, 4)].reshape(4 * HD, HD)

    def chunk_b(buf, g):
        base = (g // 2) * 8 + g % 2
        return jnp.concatenate([buf[base + 2 * dxi] for dxi in range(4)], axis=0)

    def over(body, init, groups):
        for first, count in groups:
            init = lax.fori_loop(0, count, lambda i, v: body(first + i, v), init)
        return init

    q_own = qa[0]

    def score(g, top):
        s = nt(q_own, chunk_a(ka, g))
        for b in range(4):
            tile = s[:, b * HD:(b + 1) * HD] * SCALE2 + bias_of(mask_ref[own_seg, place(g, b)])
            s_scr[g * 4 + b] = tile
            top = jnp.maximum(top, tile)
        return top

    top = jnp.full((HD, HD), MASKED_SCORE, F32)

    keys.first()
    vals.wave(1)
    vals.relay(0)
    top = over(score, top, [(0, 1)])
    keys.wave(1)
    vals.wave(2)
    vals.relay(1)
    top = over(score, top, [(2, 2)])
    keys.wave(2)
    vals.wave(3)
    vals.relay(2)
    vals.share(1)
    ques.first()
    grads.wave(1)
    grads.relay(0)
    arrive(keys.sib[0])
    top = over(score, top, [(4, 2), (10, 2)])
    keys.wave(3)
    vals.wave(4)
    vals.relay(3)
    vals.share(2)
    vals.relay(4)
    arrive(keys.sib[1])
    top = over(score, top, [(6, 2), (12, 2)])
    keys.last()
    ques.wave(1)
    grads.wave(2)
    grads.relay(1)
    vals.share(3)
    vals.share(0)
    arrive(keys.sib[2], keys.sib[3])
    top = over(score, top, [(1, 1), (14, 2), (8, 2)])
    row_top = jnp.max(top, axis=1, keepdims=True)
    w_sib = []
    for dz in range(1, nz):
        arrive(w_in[dz - 1])
        w_sib.append(send(w_all.at[dz, part], w_all.at[dz, part], sib))
    arrive(*vals.sib)

    def weigh(g, carry):
        total, attended = carry
        tiles = []
        for b in range(4):
            p = jnp.exp2(s_scr[g * 4 + b] - row_top)
            total = total + p
            tiles.append(p.astype(BF))
            p_scr[g * 4 + b] = tiles[-1]
        return total, attended + nn(jnp.concatenate(tiles, axis=1), chunk_b(vb, g))

    zero = jnp.zeros((HD, HD), F32)
    total, attended = over(weigh, (zero, zero), [(0, 16)])
    row_sum = jnp.sum(total, axis=1, keepdims=True)
    inverse = 1.0 / row_sum
    att_own = (attended * inverse).astype(BF)
    grad = ob[0]
    row_delta = jnp.sum(grad.astype(F32) * att_own.astype(F32), axis=1, keepdims=True)
    row_lse = row_top + jnp.log2(row_sum)
    lane = lax.broadcasted_iota(jnp.int32, (HD, HD), 1)
    stat[0] = jnp.where(lane == 0, row_lse, jnp.where(lane == 1, row_delta, 0.0)).T[:8]
    att[0] = att_own
    s_line = []
    for cc in (0, 1):
        for dxi, who in ((0, 0), (2, 1), (1, -1), (3, 2)):
            if cc or dxi:
                s_line.append(send(stat.at[0], stat.at[4 * cc + dxi], at(dx=who, core=cc)))
    att_in = [send(att.at[0], att.at[dz], at(dz=-dz + nz)) for dz in range(1, nz)]

    ques.wave(2)
    grads.wave(3)
    grads.relay(2)
    grads.share(1)

    def slope(g, dq):
        d = nt(grad, chunk_b(vb, g))
        tiles = [
            (p_scr[g * 4 + b].astype(F32) * (d[:, b * HD:(b + 1) * HD] - row_delta)).astype(BF) for b in range(4)
        ]
        return dq + nn(jnp.concatenate(tiles, axis=1), chunk_a(ka, g))

    dq = over(slope, zero, [(0, 8)])
    arrive(*s_line)
    s_col = []
    for d in range(1, NY):
        slot = 1 if d == 4 else (2 * d + 1 if d < 4 else 2 * (NY - d))
        s_col.append(send(rows(stat, 0, 8), rows(stat, 8 * slot, 8), at(dy=d)))
    ques.wave(3)
    grads.wave(4)
    grads.relay(3)
    grads.share(2)
    grads.relay(4)
    dq = over(slope, dq, [(8, 8)])
    dq_ref[...] = (dq * (inverse * SCALE)).astype(BF)

    ques.last()
    grads.share(3)
    grads.share(0)

    k_own, v_own = ka[0], vb[0]

    def column(g, carry):
        dk, dv = carry
        queries, ograds = chunk_a(qa, g), chunk_b(ob, g)
        s, d = nt(k_own, queries), nt(v_own, ograds)
        probs, slopes = [], []
        for b in range(4):
            st = stat[(g % 8) * 8 + (g // 8) * 4 + b]
            shift = bias_of(mask_ref[place(g, b), own_seg]) - st[0:1]
            p = jnp.exp2(s[:, b * HD:(b + 1) * HD] * SCALE2 + shift)
            probs.append(p.astype(BF))
            slopes.append((p * (d[:, b * HD:(b + 1) * HD] - st[1:2])).astype(BF))
        dk = dk + nn(jnp.concatenate(slopes, axis=1), queries)
        dv = dv + nn(jnp.concatenate(probs, axis=1), ograds)
        return dk, dv

    arrive(*s_col)
    dkv = over(column, (zero, zero), [(0, 8)])
    arrive(*ques.sib, *grads.sib)
    dk, dv = over(column, dkv, [(8, 8)])
    dk_ref[...] = (dk * SCALE).astype(BF)
    dv_ref[...] = dv.astype(BF)

    out = nt(att_own, w_own[pl.ds(pl.multiple_of(z * ow, 16), ow)])
    arrive(*w_sib, *att_in)
    for dz in range(1, nz):
        out = out + nt(att[dz], w_all[dz])
    out_ref[...] = out.astype(BF)
    for cp in sent:
        cp.wait_send()


def solution(mesh):
    nz = mesh.shape["head"]

    def local(queries, keys, values, out_weight, output_cotangent, block_mask, segment_of_device):
        width = out_weight.shape[0]
        ow = width // nz
        anywhere, vmem, smem = (pl.BlockSpec(memory_space=m) for m in (pl.ANY, pltpu.VMEM, pltpu.SMEM))
        block = jax.ShapeDtypeStruct((HD, HD), BF)
        buf = pltpu.VMEM((BLOCKS, HD, HD), BF)
        return pl.pallas_call(
            functools.partial(kernel, nz, ow),
            out_shape=(jax.ShapeDtypeStruct((HD, ow), BF), block, block, block),
            in_specs=[anywhere] * 5 + [smem] * 2,
            out_specs=(vmem,) * 4,
            scratch_shapes=[
                buf, buf, buf, buf,
                pltpu.VMEM((BLOCKS, HD, HD), F32),
                pltpu.VMEM((BLOCKS, HD, HD), BF),
                pltpu.VMEM((width, HD), BF),
                pltpu.VMEM((HD, width), BF),
                pltpu.VMEM((nz, ow, HD), BF),
                pltpu.VMEM((nz, HD, HD), BF),
                pltpu.VMEM((BLOCKS, 8, HD), F32),
                pltpu.SemaphoreType.DMA((8,)),
                pltpu.SemaphoreType.DMA((160,)),
                pltpu.SemaphoreType.DMA((160,)),
            ],
            compiler_params=pltpu.CompilerParams(
                collective_id=0, has_side_effects=True, vmem_limit_bytes=48 * 1024 * 1024
            ),
        )(queries, keys, values, out_weight, output_cotangent, block_mask, segment_of_device)

    return jax.shard_map(
        local,
        mesh=mesh,
        in_specs=(P("tm", "head"), P("tm", "head"), P("tm", "head"), P(None, "head"), P("tm", None), P(), P()),
        out_specs=(P("tm", "head"), P("tm", "head"), P("tm", "head"), P("tm", "head")),
        check_vma=False,
    )
```

time: 399 us -> 80.9 us (0.20)
  waiting for transfers between devices: 275 us -> 0 us
  Pallas kernels: 0 us -> 70.9 us
  blocking collectives: 68 us -> 0 us
  matrix products: 32.6 us -> 0 us
  between operations: 13.9 us -> 0.66 us
  local copies, waits for them, and re-layouts: 3.96 us -> 8.82 us
    all_gather x4 -> x0, waiting for transfers between devices: 249 us -> none  [the longest x1 85.8 us: local(): key_piece = lax.all_gather(keys, 'tm', axis=0, tiled=True)]
    pallas_call x0 -> x1, Pallas kernels: none -> 70.9 us  [local(): pl.pallas_call(functools.partial(kernel, nz, ow), out_shape=(jax.ShapeDty...]
    all_gather x2 -> x0, blocking collectives: 68 us -> none  [the longest x1 34.1 us: local(): delta_piece = lax.all_gather(row_delta, 'tm', axis=0, tiled=True)]
    dot_general x10 -> x0, matrix products: 32.6 us -> none  [the longest x2 10.6 us: row_products(): lax.dot_general(left, right, (((0,), (0,)), ((), ())), preferred_element_...]
    unnamed x6 -> x0, waiting for transfers between devices: 26 us -> none
    unnamed x20 -> x18, local copies, waits for them, and re-layouts: 3.96 us -> 8.82 us
  transfers between devices with their start and end apart: 5 -> 0, of which waited for: 5 -> 0; matrix products, arithmetic and copies ran while one was open for 9% -> 0% of each run, Pallas kernels for 0% -> 0%
where the time goes in v1:
time: 80.9 us; the launch traced here: 80.4 us
  Pallas kernels  70.9 us (88%)
  local copies, waits for them, and re-layouts  8.82 us (11%)
    pallas_call x1, Pallas kernels, local(): pl.pallas_call(functools.partial(kernel, nz, ow), out_shape=(jax.ShapeDty...  70.9 us
    unnamed x18, local copies, waits for them, and re-layouts  8.82 us

profile of v1, /device:TPU:1, one launch (start us, length us, event | category | flops | bytes accessed | tf_op | source)
XLA Modules:
  0.0 80.4 jit_solution(13666037218131426380)
XLA Ops:
  0.6 0.0 copy-start
  0.6 1.3 %copy-done = bf16[5120,128]{1,0:T(8,128)(2,1)S(1)} copy-done((bf16[5120,128]{1,0:T(8,128)(2,1)S(1)}, bf16[5120,128]{1,0:T(8,128)(2,1)}, u32[]{:S(2)}) %copy-start) | copy-done | bytes 1310744
  2.0 0.0 copy-start.1
  2.0 1.3 %copy-done.1 = bf16[128,5120]{1,0:T(8,128)(2,1)S(1)} copy-done((bf16[128,5120]{1,0:T(8,128)(2,1)S(1)}, bf16[128,5120]{1,0:T(8,128)(2,1)}, u32[]{:S(2)}) %copy-start.1) | copy-done | bytes 1310744
  3.3 0.0 copy-start.2
  3.3 0.8 copy-done.2
  4.0 0.0 copy-start.3
  4.0 0.8 copy-done.3
  4.8 0.0 copy-start.4
  4.8 0.8 copy-done.4
  5.5 0.0 copy-start.5
  5.5 0.8 copy-done.5
  6.3 0.0 copy-start.6
  6.3 0.7 copy-done.6
  7.0 70.9 %shard_map.102 = (bf16[128,640]{1,0:T(8,128)(2,1)S(1)}, bf16[128,128]{1,0:T(8,128)(2,1)S(1)}, bf16[128,128]{1,0:T(8,128)(2,1)S(1)}, bf16[128,128]{1,0:T(8,128)(2,1)S(1)}) custom-call(bf16[128,128]{1,0:T(8,128)(2,1)S(1)} %copy-done.2, bf16[128,128]{1,0:T(8,128)(2,1)S(1)} %copy-done.3, bf16[128,128]{1,0:T(8,128)(2,1)S(1)} %copy-done.4, ...), custom_call_target="tpu_custom_call" | custom-call | tf_op jit(solution)/shard_map/pallas_call | solution.py:332
  77.9 0.7 copy.15
  78.6 0.6 copy.16
  79.2 0.6 copy.17
  79.8 0.6 copy.18
Async XLA Ops:
  0.6 1.3 %copy-start = (bf16[5120,128]{1,0:T(8,128)(2,1)S(1)}, bf16[5120,128]{1,0:T(8,128)(2,1)}, u32[]{:S(2)}) copy-start(bf16[5120,128]{1,0:T(8,128)(2,1)} %w_hbm.1) | copy-start | bytes 3932164
  2.0 1.3 %copy-start.1 = (bf16[128,5120]{1,0:T(8,128)(2,1)S(1)}, bf16[128,5120]{1,0:T(8,128)(2,1)}, u32[]{:S(2)}) copy-start(bf16[128,5120]{1,0:T(8,128)(2,1)} %cot_hbm.1) | copy-start | bytes 3932164
  3.3 0.8 copy-start.2
  4.0 0.8 copy-start.3
  4.8 0.8 copy-start.4
  5.5 0.8 copy-start.5
  6.3 0.7 copy-start.6

commit v2 on v0

v2 whole, which is shorter than its diff:
```python
import functools
import math

import jax
import jax.numpy as jnp
from jax import lax
from jax.experimental import pallas as pl
from jax.experimental.pallas import tpu as pltpu
from jax.sharding import PartitionSpec as P

HD = 128
NX, NY = 4, 8
BLOCKS = 2 * NX * NY
MASKED_SCORE = -1e30
SCALE = 1.0 / math.sqrt(HD)
SCALE2 = SCALE * math.log2(math.e)
MESH = pl.DeviceIdType.MESH
BF, F32 = jnp.bfloat16, jnp.float32

DX = (0, 1, -1, 2)
RIGHT, LEFT, ACROSS, UP, DOWN, SIB = (1, 0, 0), (-1, 0, 0), (2, 0, 0), (0, 1, 0), (0, -1, 0), (0, 0, 1)
TOP, LOW = pl.ds(0, 64), pl.ds(64, 64)
WAVES = (1, 2, 3, 0)

ROUTES = ((0, 1, True), (1, 0.5, 0), (0, 3, True), (1, 2.5, 1))
ORDER = (
    "Vy1 Vx0 Ky10 Kl", "Qy10 Gy2 Gx0 Ql", "Vy2 Vx1 Vr0 Ky20", "Ky12 Ky11 Ky13 Gr0",
    "Gx2 Vx2 Vy3 W", "Ky30 Ky22 Vr1 Ky21", "Ks1 Ky23 Vx3 Vy4", "Qy12 Ky40 Gr2 score1",
    "Qy20 Vr2 Ky32 Ky31", "Vs1 Ky33 Ks2 Vx4", "Vr3 Kf pv1 Gy3", "Gs2 score2 Vs2 Qy30",
    "Vr4 Gy1 Vs3 Ks3", "Qy13 pv2 Qy11 Gx4", "Qy22 Ks0 Gx3 Vs0", "Qy40 score3 Gx1 pv3",
    "Qy23 score0 Qy21 Gr4", "Qs1 pv0 stat Qf", "att Qy32 slope1 slope3", "Gr1 Qy33 Gs0 slope2",
    "Qs2 Qy31 Gr3 slope0", "dq scol Qs0 pre2", "Gs1 Gs3 Qs3 pre0", "pre1 col2 col0 w4",
    "w7 w3 w5 w2", "w6 w1 col1 pre3", "col3 dkv out",
)


class Route:
    def __init__(self, name, buf, post, send, rank):
        self.name, self.buf, self.rank = name, buf, rank
        self.post, self.send = post, send
        self.need, self.sib = {}, {}

    def move(self, src, dst, count, who, half=None):
        if half is not None:
            return self.send(self.buf, (src, half), (dst, half), who, count * 0.5)
        return self.send(self.buf, (pl.ds(src, count),), (pl.ds(dst, count),), who, count)

    def task(self, label, waits, work, rank=0.0):
        self.post(self.name + label, waits, work, self.rank + rank)

    def share(self):
        for p in WAVES:
            def work(p=p):
                return [self.move(8 * p, 32 + 8 * p, 8, SIB)]
            self.task("s%d" % p, self.need[p], work, 0.2)
            self.need[p] = self.need[p] + [self.name + "s%d.0" % p]


class RouteA(Route):
    def __init__(self, name, buf, post, send, rank, ready=(), far=False):
        super().__init__(name, buf, post, send, rank)
        ready, move = list(ready), self.move
        self.task("l", ready, lambda: [move(0, 2, 1, RIGHT), move(0, 1, 1, LEFT), move(0, 3, 1, ACROSS)])
        line = [ready, [name + "l.1"], [name + "l.0"], [name + "l.2"]]
        for p in (1, 2, 3):
            self.need[p] = []
        for d in range(4):
            def first(d=d):
                return [move(d, 12 + d, 1, UP), move(d, 8 + d, 1, DOWN)]
            self.task("y1%d" % d, line[d], first, 0.1)
            for p in (1, 2, 3):
                got = ["%sy%d%d.%d" % (name, p, d, i) for i in (0, 1)]
                self.need[p] += got
                if p < 3:
                    def more(d=d, g=8 * p):
                        return [move(g + 4 + d, g + 12 + d, 1, UP), move(g + d, g + 8 + d, 1, DOWN)]
                elif far and d:
                    continue
                elif far:
                    def more():
                        return [move(28, 4, 1, UP, TOP), move(24, 4, 1, DOWN, LOW)]
                else:
                    def more(d=d):
                        return [move(28 + d, 4 + d, 1, UP) if d < 2 else move(24 + d, 4 + d, 1, DOWN)]
                self.task("y%d%d" % (p + 1, d), got, more, 0.1)
        if far:
            self.task(
                "f", [name + "y40.0", name + "y40.1"],
                lambda: [move(4, 6, 1, RIGHT), move(4, 5, 1, LEFT), move(4, 7, 1, ACROSS)], 0.1
            )
            last = [name + "f.%d" % i for i in range(3)] + [name + "y40.0", name + "y40.1"]
        else:
            last = [name + "y4%d.0" % d for d in range(4)]
        self.need[0] = line[1] + line[2] + line[3] + last
        self.share()


class RouteB(Route):
    def __init__(self, name, buf, post, send, rank, ready=(), mode=0):
        super().__init__(name, buf, post, send, rank)
        ready, move = list(ready), self.move

        def to(p, src=0):
            return [move(src, 8 * p + 1, 1, (0, p, 0)), move(src, 8 * p, 1, (0, -p, 0))]

        got = {}
        if mode == 0:
            self.task("y1", ready, lambda: to(1))
            got[1] = [name + "y1.0", name + "y1.1"]
            for p in (1, 2, 3):
                if p < 3:
                    def work(g=8 * p):
                        return [move(g + 1, g + 9, 1, UP), move(g, g + 8, 1, DOWN)]
                else:
                    def work():
                        return [move(25, 1, 1, UP, TOP), move(24, 1, 1, DOWN, LOW)]
                self.task("y%d" % (p + 1), got[p], work)
                got[p + 1] = ["%sy%d.%d" % (name, p + 1, i) for i in (0, 1)]
        elif mode == 1:
            self.task("y2", ready, lambda: to(2))
            self.task("y1", ready, lambda: to(1), 0.01)
            got[1], got[2] = [name + "y1.0", name + "y1.1"], [name + "y2.0", name + "y2.1"]

            def work():
                return [
                    move(17, 1, 1, (0, 2, 0), TOP), move(16, 1, 1, (0, -2, 0), LOW),
                    move(17, 25, 1, UP), move(16, 24, 1, DOWN),
                ]
            self.task("y3", got[2], work)
            got[4], got[3] = [name + "y3.0", name + "y3.1"], [name + "y3.2", name + "y3.3"]
        else:
            self.task("y4", ready, lambda: [move(0, 1, 1, (0, 4, 0))])
            got[4] = [name + "y4.0"]
            for p in (3, 2, 1):
                self.task("y%d" % p, ready, lambda p=p: to(p), 0.01)
                got[p] = ["%sy%d.%d" % (name, p, i) for i in (0, 1)]
        got[0] = ready
        for p in (0, 1, 2, 3, 4):
            g, k, n = (8 * p, 0, 2) if 1 <= p <= 3 else (0, p // 4, 1)

            def cross(g=g, k=k, n=n):
                return [move(g + k, g + 4 + k, n, RIGHT), move(g + k, g + 2 + k, n, LEFT)]

            def relay(g=g, k=k, n=n):
                if n == 2:
                    return [move(g + 4, g + 6, 1, RIGHT), move(g + 3, g + 7, 1, LEFT)]
                return [move(4 + k, 6 + k, 1, RIGHT, TOP), move(2 + k, 6 + k, 1, LEFT, LOW)]

            self.task("x%d" % p, got[p], cross, 0.02)
            near = ["%sx%d.%d" % (name, p, i) for i in (0, 1)]
            self.task("r%d" % p, near, relay, 0.05)
            mine = (got[p] if p else []) + near + ["%sr%d.%d" % (name, p, i) for i in (0, 1)]
            self.need[p % 4] = self.need.get(p % 4, []) + mine
        self.share()


def routes(post, send, bufs, ready):
    made = []
    for (kind, rank, option), name, buf, dep in zip(ROUTES, "KVQG", bufs, ready):
        if kind:
            made.append(RouteB(name, buf, post, send, rank, dep, option))
        else:
            made.append(RouteA(name, buf, post, send, rank, dep, option))
    return [r.need for r in made]


def work_plan(post, send, bufs, act, nz):
    keys, vals, ques, grads = routes(post, send, bufs, ((), (), (), ()))
    w_in = []
    if nz > 1:
        post("W", ["Ky20.0"], act("W", 0), 0.9)
        for dz in range(1, nz):
            post("w%d" % dz, ["scol", "W.%d" % (dz - 1)], act("w", dz), 9.5)
            w_in += ["W.%d" % (dz - 1), "w%d.0" % dz]
    for p in WAVES:
        post("score%d" % p, keys[p], act("score", p), 10)
        post("pv%d" % p, vals[p] + ["score%d" % p], act("pv", p), 10.5)
        post("pre%d" % p, ques[p] + grads[p], act("pre", p), 13)
    post("stat", ["pv%d" % p for p in WAVES], act("stat", 0), 5)
    line = ["stat.%d" % i for i in range(7)]
    post("scol", line, act("scol", 0), 0)
    col = line + ["scol.%d" % i for i in range(NY - 1)]
    for p in WAVES:
        post("slope%d" % p, ["stat"], act("slope", p), 14)
        post("col%d" % p, col + ["pre%d" % p], act("col", p), 12)
    post("dq", ["slope%d" % p for p in WAVES], act("dq", 0), 15)
    post("dkv", ["col%d" % p for p in WAVES], act("dkv", 0), 11)
    if nz > 1:
        post("att", ["stat"], act("att", 0), 5.5)
    post("out", ["stat"] + w_in + ["att.%d" % i for i in range(nz - 1)], act("out", 0), 20)


def nt(left, right):
    return lax.dot_general(left, right, (((1,), (1,)), ((), ())), preferred_element_type=F32)


def nn(left, right):
    return lax.dot_general(left, right, (((1,), (0,)), ((), ())), preferred_element_type=F32)


def kernel(nz, ow, q_hbm, k_hbm, v_hbm, w_hbm, cot_hbm, mask_ref, seg_ref, out_ref, dq_ref, dk_ref, dv_ref,
           ka, vb, qa, ob, p_scr, s_scr, d_scr, w_own, cot, w_all, att, stat, lsem, ssem, rsem, go_sem):
    t, z = lax.axis_index("tm"), lax.axis_index("head")
    y, x, c = t // (2 * NX), (t // 2) % NX, t % 2

    def at(dx=0, dy=0, core=0, dz=0):
        col, row = (x + (dx + NX)) % NX, (y + (dy + NY)) % NY
        return ((row * NX + col) * 2 + (c + core) % 2, (z + (dz + nz)) % nz)

    loads = []
    for src, dst in ((w_hbm, w_own), (cot_hbm, cot), (k_hbm, ka.at[0]), (v_hbm, vb.at[0]), (q_hbm, qa.at[0])):
        cp = pltpu.make_async_copy(src, dst, lsem.at[len(loads)])
        cp.start()
        loads.append(cp)

    def signal(sem, who):
        pl.semaphore_signal(sem, inc=1, device_id=who, device_id_type=MESH)

    barrier = pltpu.get_barrier_semaphore()
    chips = [(dx, 0) for dx in DX[1:]] + [(0, dy) for dy in range(1, NY)]
    for dx, dy in chips:
        signal(barrier, at(dx, dy, c))

    @pl.when(c == 1)
    def _():
        signal(barrier, at(core=1))

    for cp in loads[:2]:
        cp.wait()
    grad = nn(cot[...], w_own[...]).astype(BF)
    ob[0] = grad
    for cp in loads[2:]:
        cp.wait()

    @pl.when(c == 0)
    def _():
        pl.semaphore_wait(barrier, 2 * len(chips) + 1)
        signal(go_sem, at(core=1))

    @pl.when(c == 1)
    def _():
        pl.semaphore_wait(go_sem, 1)
        for dz in range(1, nz):
            signal(barrier, at(dz=dz))

    sent, val = [], {}

    def push(src, dst, who):
        i = len(sent)
        cp = pltpu.make_async_remote_copy(
            src_ref=src, dst_ref=dst, send_sem=ssem.at[i], recv_sem=rsem.at[i], device_id=who, device_id_type=MESH
        )
        cp.start()
        sent.append(cp)
        return cp

    def send(buf, src, dst, who, count):
        return push(buf.at[src], buf.at[dst], at(*who))

    q_own, k_own, v_own = qa[0], ka[0], vb[0]
    own_seg = seg_ref[t]
    half = ow // 2
    part = pl.ds(pl.multiple_of(c * half, 16), half)

    def cells(p):
        return [(core, k, dxi) for core in (0, 1) for k in (0, 1) for dxi in range(4)]

    def place(p, core, k, dxi):
        dy = (4 * k) if p == 0 else (p if k == 0 else NY - p)
        col, row = (x + (DX[dxi] + NX)) % NX, (y + dy) % NY
        return seg_ref[(row * NX + col) * 2 + (c + core) % 2]

    def bias_of(link):
        return (1 - link).astype(F32) * MASKED_SCORE

    def chunk_a(buf, p):
        return jnp.concatenate([buf[pl.ds(32 * core + 8 * p, 8)].reshape(8 * HD, HD) for core in (0, 1)], axis=0)

    def chunk_b(buf, p):
        return jnp.concatenate([buf[32 * core + 8 * p + 2 * dxi + k] for core, k, dxi in cells(p)], axis=0)

    def score(p):
        s = nt(q_own, chunk_a(ka, p))
        tiles = []
        for i, cell in enumerate(cells(p)):
            bias = bias_of(mask_ref[own_seg, place(p, *cell)])
            tiles.append(s[:, i * HD:(i + 1) * HD] * SCALE2 + bias)
        top = functools.reduce(jnp.maximum, tiles)
        top = jnp.max(top, axis=1, keepdims=True)
        tiles = [jnp.exp2(tile - top) for tile in tiles]
        total = jnp.sum(functools.reduce(jnp.add, tiles), axis=1, keepdims=True)
        for i, tile in enumerate(tiles):
            p_scr[p * 16 + i] = tile.astype(BF)
        val["top", p], val["sum", p] = top, total

    def pv(p):
        val["pv", p] = nn(jnp.concatenate([p_scr[p * 16 + i] for i in range(16)], axis=1), chunk_b(vb, p))

    def finish(_):
        tops = [val["top", p] for p in WAVES]
        top = functools.reduce(jnp.maximum, tops)
        scale = {p: jnp.exp2(val["top", p] - top) for p in WAVES}
        row_sum = sum(val["sum", p] * scale[p] for p in WAVES)
        inverse = 1.0 / row_sum
        attended = (sum(val["pv", p] * scale[p] for p in WAVES) * inverse).astype(BF)
        delta = jnp.sum(grad.astype(F32) * attended.astype(F32), axis=1, keepdims=True)
        lse = top + jnp.log2(row_sum)
        lane = lax.broadcasted_iota(jnp.int32, (HD, HD), 1)
        stat[0] = jnp.where(lane == 0, lse, jnp.where(lane == 1, delta, 0.0)).T[:2]
        att[0] = attended
        val["att"], val["delta"] = attended, delta
        for p in WAVES:
            val["f", p] = scale[p] * (inverse * SCALE)
        return [
            push(stat.at[0], stat.at[4 * core + slot], at(dx=dx, core=core))
            for core in (0, 1) for slot, dx in ((0, 0), (2, 1), (1, -1), (3, 2)) if core or slot
        ]

    def spread(_):
        out = []
        for d in (4, 3, 5, 2, 6, 1, 7):
            slot = 1 if d == 4 else (2 * d + 1 if d < 4 else 2 * (NY - d))
            out.append(push(stat.at[pl.ds(0, 8)], stat.at[pl.ds(8 * slot, 8)], at(dy=d)))
        return out

    def slope(p):
        d = nt(grad, chunk_b(vb, p))
        tiles = [
            (p_scr[p * 16 + i].astype(F32) * (d[:, i * HD:(i + 1) * HD] - val["delta"])).astype(BF) for i in range(16)
        ]
        val["dq", p] = nn(jnp.concatenate(tiles, axis=1), chunk_a(ka, p)) * val["f", p]

    def put_dq(_):
        dq_ref[...] = sum(val["dq", p] for p in WAVES).astype(BF)

    def pre(p):
        s, d = nt(k_own, chunk_a(qa, p)), nt(v_own, chunk_b(ob, p))
        for i, cell in enumerate(cells(p)):
            bias = bias_of(mask_ref[place(p, *cell), own_seg])
            s_scr[p * 16 + i] = s[:, i * HD:(i + 1) * HD] * SCALE2 + bias
            d_scr[p * 16 + i] = d[:, i * HD:(i + 1) * HD]

    def col(p):
        probs, slopes = [], []
        for i, (core, k, dxi) in enumerate(cells(p)):
            st = stat[(2 * p + k) * 8 + core * 4 + dxi]
            e = jnp.exp2(s_scr[p * 16 + i] - st[0:1])
            probs.append(e.astype(BF))
            slopes.append((e * (d_scr[p * 16 + i] - st[1:2])).astype(BF))
        dk = nn(jnp.concatenate(slopes, axis=1), chunk_a(qa, p))
        dv = nn(jnp.concatenate(probs, axis=1), chunk_b(ob, p))
        val["dk"] = val["dk"] + dk if "dk" in val else dk
        val["dv"] = val["dv"] + dv if "dv" in val else dv

    def put_dkv(_):
        dk_ref[...] = (val["dk"] * SCALE).astype(BF)
        dv_ref[...] = val["dv"].astype(BF)

    def weights(_):
        out = []

        @pl.when(c == 1)
        def _():
            pl.semaphore_wait(barrier, nz - 1)
            signal(go_sem, at(core=1))

        @pl.when(c == 0)
        def _():
            pl.semaphore_wait(go_sem, 1)

        for dz in range(1, nz):
            first = pl.multiple_of(((z + nz - dz) % nz) * ow + c * half, 16)
            out.append(push(w_own.at[pl.ds(first, half)], w_all.at[dz, part], at(dz=-dz)))
        return out

    def weight(dz):
        return [push(w_all.at[dz, part], w_all.at[dz, part], at(core=1))]

    def heads(_):
        return [push(att.at[0], att.at[dz], at(dz=-dz)) for dz in range(1, nz)]

    def project(_):
        out = nt(val["att"], w_own[pl.ds(pl.multiple_of(z * ow, 16), ow)])
        for dz in range(1, nz):
            out = out + nt(att[dz], w_all[dz])
        out_ref[...] = out.astype(BF)

    acts = {
        "score": score, "pv": pv, "pre": pre, "stat": finish, "scol": spread, "slope": slope, "col": col, "dq": put_dq,
        "dkv": put_dkv, "W": weights, "w": weight, "att": heads, "out": project,
    }
    tasks = {}

    def post(name, waits, work, rank):
        tasks[name] = (waits, work)

    work_plan(post, send, (ka, vb, qa, ob), lambda kind, i: functools.partial(acts[kind], i), nz)
    names = [n for n in " ".join(ORDER).split() if n in tasks]
    assert sorted(names) == sorted(tasks)
    coming = {}
    for name in names:
        waits, work = tasks[name]
        for dep in waits:
            if "." in dep and coming[dep] is not None:
                coming[dep].wait_recv()
                coming[dep] = None
            elif "." not in dep:
                assert dep in tasks and names.index(dep) < names.index(name)
        for i, cp in enumerate(work() or ()):
            coming["%s.%d" % (name, i)] = cp
    assert all(cp is None for cp in coming.values())
    for cp in sent:
        cp.wait_send()


def hand_over(*refs):
    for i in range(4):
        refs[4 + i][...] = refs[i][...]


def solution(mesh):
    nz = mesh.shape["head"]

    def local(queries, keys, values, out_weight, output_cotangent, block_mask, segment_of_device):
        width = out_weight.shape[0]
        ow = width // nz
        anywhere, vmem, smem = (pl.BlockSpec(memory_space=m) for m in (pltpu.HBM, pltpu.VMEM, pltpu.SMEM))
        block = jax.ShapeDtypeStruct((HD, HD), BF)
        buf, big = pltpu.VMEM((BLOCKS, HD, HD), BF), pltpu.VMEM((BLOCKS, HD, HD), F32)
        shapes = (jax.ShapeDtypeStruct((HD, ow), BF), block, block, block)
        results = pl.pallas_call(
            functools.partial(kernel, nz, ow),
            out_shape=shapes,
            in_specs=[anywhere] * 5 + [smem] * 2,
            out_specs=(vmem,) * 4,
            scratch_shapes=[
                buf, buf, buf, buf, buf, big, big,
                pltpu.VMEM((width, HD), BF),
                pltpu.VMEM((HD, width), BF),
                pltpu.VMEM((nz, ow, HD), BF),
                pltpu.VMEM((nz, HD, HD), BF),
                pltpu.VMEM((BLOCKS, 2, HD), F32),
                pltpu.SemaphoreType.DMA((8,)),
                pltpu.SemaphoreType.DMA((240,)),
                pltpu.SemaphoreType.DMA((240,)),
                pltpu.SemaphoreType.REGULAR,
            ],
            compiler_params=pltpu.CompilerParams(
                collective_id=0, has_side_effects=True, vmem_limit_bytes=64 * 1024 * 1024
            ),
        )(queries, keys, values, out_weight, output_cotangent, block_mask, segment_of_device)
        return pl.pallas_call(
            hand_over,
            out_shape=shapes,
            in_specs=[vmem] * 4,
            out_specs=(vmem,) * 4,
            compiler_params=pltpu.CompilerParams(vmem_limit_bytes=64 * 1024 * 1024),
        )(*results)

    return jax.shard_map(
        local,
        mesh=mesh,
        in_specs=(P("tm", "head"), P("tm", "head"), P("tm", "head"), P(None, "head"), P("tm", None), P(), P()),
        out_specs=(P("tm", "head"), P("tm", "head"), P("tm", "head"), P("tm", "head")),
        check_vma=False,
    )
```

time: 399 us -> 56.2 us (0.14)
  waiting for transfers between devices: 275 us -> 0 us
  blocking collectives: 68 us -> 0 us
  Pallas kernels: 0 us -> 55.3 us
  matrix products: 32.6 us -> 0 us
  between operations: 13.9 us -> 0.64 us
    all_gather x4 -> x0, waiting for transfers between devices: 249 us -> none  [the longest x1 85.8 us: local(): key_piece = lax.all_gather(keys, 'tm', axis=0, tiled=True)]
    all_gather x2 -> x0, blocking collectives: 68 us -> none  [the longest x1 34.1 us: local(): delta_piece = lax.all_gather(row_delta, 'tm', axis=0, tiled=True)]
    pallas_call x0 -> x2, Pallas kernels: none -> 55.3 us  [the longest x1 53.6 us: local(): pl.pallas_call(functools.partial(kernel, nz, ow), out_shape=shapes, in_sp...]
    dot_general x10 -> x0, matrix products: 32.6 us -> none  [the longest x2 10.6 us: row_products(): lax.dot_general(left, right, (((0,), (0,)), ((), ())), preferred_element_...]
    unnamed x6 -> x0, waiting for transfers between devices: 26 us -> none
  transfers between devices with their start and end apart: 5 -> 0, of which waited for: 5 -> 0; matrix products, arithmetic and copies ran while one was open for 9% -> 0% of each run, Pallas kernels for 0% -> 0%
where the time goes in v2:
time: 56.2 us; the launch traced here: 55.9 us
  Pallas kernels  55.3 us (98%)
  between operations  0.64 us (1%)
    pallas_call x1, Pallas kernels, local(): pl.pallas_call(functools.partial(kernel, nz, ow), out_shape=shapes, in_sp...  53.6 us
    pallas_call x1, Pallas kernels, local(): pl.pallas_call(hand_over, out_shape=shapes, in_specs=[vmem] * 4, out_spec...  1.64 us

profile of v2, /device:TPU:1, one launch (start us, length us, event | category | flops | bytes accessed | tf_op | source)
XLA Modules:
  0.0 55.9 jit_solution(13088599702455570803)
XLA Ops:
  0.6 53.6 %shard_map.102 = (bf16[128,640]{1,0:T(8,128)(2,1)}, bf16[128,128]{1,0:T(8,128)(2,1)}, bf16[128,128]{1,0:T(8,128)(2,1)}, bf16[128,128]{1,0:T(8,128)(2,1)}) custom-call(bf16[128,128]{1,0:T(8,128)(2,1)} %q_hbm.1, bf16[128,128]{1,0:T(8,128)(2,1)} %k_hbm.1, bf16[128,128]{1,0:T(8,128)(2,1)} %v_hbm.1, bf16[5120,128]{1,0:T(8,128)(2,1)} %w_hbm.1, ...), custom_call_target="tpu_custom_call" | custom-call | tf_op jit(solution)/shard_map/pallas_call | solution.py:431
  54.3 1.6 %shard_map.103 = (bf16[128,640]{1,0:T(8,128)(2,1)}, bf16[128,128]{1,0:T(8,128)(2,1)}, bf16[128,128]{1,0:T(8,128)(2,1)}, bf16[128,128]{1,0:T(8,128)(2,1)}) custom-call(bf16[128,640]{1,0:T(8,128)(2,1)} %get-tuple-element.8.refs_0_, bf16[128,128]{1,0:T(8,128)(2,1)} %get-tuple-element.9.refs_1_, bf16[128,128]{1,0:T(8,128)(2,1)} %get-tuple-element.10.refs_2_, ...), custom_call_target="tpu_custom_call" | custom-call | tf_op jit(solution)/shard_map/pallas_call | solution.py:452

commit v3 on v2

--- a/solution.py
+++ b/solution.py
@@ -22,15 +22,19 @@
 TOP, LOW = pl.ds(0, 64), pl.ds(64, 64)
 WAVES = (1, 2, 3, 0)
 
-ROUTES = ((0, 1, True), (1, 0.5, 0), (0, 3, True), (1, 2.5, 1))
+
+def far_first(nz):
+    return sorted(range(1, nz), key=lambda dz: -min(dz, nz - dz))
+
+NEAR = (1, -1, 2, -2)
+ROUTES = ((0, 1, 1), (1, 0.5, 1), (0, 3, 1), (1, 2.5, 0))
 ORDER = (
-    "Vy1 Vx0 Ky10 Kl", "Qy10 Gy2 Gx0 Ql", "Vy2 Vx1 Vr0 Ky20", "Ky12 Ky11 Ky13 Gr0",
-    "Gx2 Vx2 Vy3 W", "Ky30 Ky22 Vr1 Ky21", "Ks1 Ky23 Vx3 Vy4", "Qy12 Ky40 Gr2 score1",
-    "Qy20 Vr2 Ky32 Ky31", "Vs1 Ky33 Ks2 Vx4", "Vr3 Kf pv1 Gy3", "Gs2 score2 Vs2 Qy30",
-    "Vr4 Gy1 Vs3 Ks3", "Qy13 pv2 Qy11 Gx4", "Qy22 Ks0 Gx3 Vs0", "Qy40 score3 Gx1 pv3",
-    "Qy23 score0 Qy21 Gr4", "Qs1 pv0 stat Qf", "att Qy32 slope1 slope3", "Gr1 Qy33 Gs0 slope2",
-    "Qs2 Qy31 Gr3 slope0", "dq scol Qs0 pre2", "Gs1 Gs3 Qs3 pre0", "pre1 col2 col0 w4",
-    "w7 w3 w5 w2", "w6 w1 col1 pre3", "col3 dkv out",
+    1, 0, 40, 24, 23, 26, 63, 2, 5, 28, 67, 8, 11, 30, 25, 27, 3, 61, 64, 69, 29, 9, 12, 6,
+    81, 34, 41, 32, 15, 4, 31, 65, 71, 16, 10, 36, 13, 17, 7, 35, 18, 21, 42, 14, 48, 51, 33, 70,
+    89, 37, 66, 45, 92, 20, 90, 72, 73, 19, 43, 39, 93, 22, 49, 52, 68, 75, 38, 95, 46, 98, 44, 99,
+    96, 101, 113, 50, 76, 77, 56, 55, 74, 47, 105, 53, 54, 107, 114, 78, 58, 103, 57, 102, 109, 80, 111, 91,
+    79, 59, 94, 60, 62, 104, 84, 83, 87, 82, 86, 88, 85, 106, 97, 100, 108, 115, 110, 116, 117, 112, 119, 118,
+    120, 121, 122,
 )
 
 
@@ -48,12 +52,16 @@
     def task(self, label, waits, work, rank=0.0):
         self.post(self.name + label, waits, work, self.rank + rank)
 
-    def share(self):
+    def share(self, split):
         for p in WAVES:
-            def work(p=p):
-                return [self.move(8 * p, 32 + 8 * p, 8, SIB)]
-            self.task("s%d" % p, self.need[p], work, 0.2)
-            self.need[p] = self.need[p] + [self.name + "s%d.0" % p]
+            for i, waits in enumerate(self.need[p] if split else [self.need[p]]):
+                def work(start=8 * p + 4 * i, count=4 if split else 8):
+                    return [self.move(start, 32 + start, count, SIB)]
+                self.task("s%d%d" % (p, i), waits, work, 0.2)
+            if split:
+                self.need[p] = self.need[p][0] + self.need[p][1] + ["%ss%d%d.0" % (self.name, p, i) for i in (0, 1)]
+            else:
+                self.need[p] = self.need[p] + ["%ss%d0.0" % (self.name, p)]
 
 
 class RouteA(Route):
@@ -63,18 +71,37 @@
         self.task("l", ready, lambda: [move(0, 2, 1, RIGHT), move(0, 1, 1, LEFT), move(0, 3, 1, ACROSS)])
         line = [ready, [name + "l.1"], [name + "l.0"], [name + "l.2"]]
         for p in (1, 2, 3):
-            self.need[p] = []
-        for d in range(4):
+            self.need[p] = ([], [])
+        for d in range(4 if far == 3 else 0):
+            def two(d=d):
+                return [move(d, 20 + d, 1, (0, 2, 0)), move(d, 16 + d, 1, (0, -2, 0))]
+
+            def one(d=d):
+                return [move(d, 12 + d, 1, UP), move(d, 8 + d, 1, DOWN)]
+
+            def three(d=d):
+                return [move(20 + d, 28 + d, 1, UP), move(16 + d, 24 + d, 1, DOWN)]
+            got = ["%sy2%d.%d" % (name, d, i) for i in (0, 1)]
+            self.task("y2%d" % d, line[d], two, 0.1)
+            self.task("y1%d" % d, line[d], one, 0.11)
+            self.task("y3%d" % d, got, three, 0.1)
+            for p in (1, 2, 3):
+                for i in (0, 1):
+                    self.need[p][1 - i].append("%sy%d%d.%d" % (name, p, d, i))
+        for d in range(0 if far == 3 else 4):
             def first(d=d):
                 return [move(d, 12 + d, 1, UP), move(d, 8 + d, 1, DOWN)]
             self.task("y1%d" % d, line[d], first, 0.1)
             for p in (1, 2, 3):
                 got = ["%sy%d%d.%d" % (name, p, d, i) for i in (0, 1)]
-                self.need[p] += got
+                for i in (0, 1):
+                    self.need[p][1 - i].append(got[i])
                 if p < 3:
                     def more(d=d, g=8 * p):
                         return [move(g + 4 + d, g + 12 + d, 1, UP), move(g + d, g + 8 + d, 1, DOWN)]
                 elif far and d:
+                    continue
+                elif far == 2:
                     continue
                 elif far:
                     def more():
@@ -84,15 +111,18 @@
                         return [move(28 + d, 4 + d, 1, UP) if d < 2 else move(24 + d, 4 + d, 1, DOWN)]
                 self.task("y%d%d" % (p + 1, d), got, more, 0.1)
         if far:
+            end = [name + "y40.0", name + "y40.1"][:1 if far > 1 else 2]
+            if far > 1:
+                self.task("y40", ready, lambda: [move(0, 4, 1, (0, 4, 0))], 0.15)
             self.task(
-                "f", [name + "y40.0", name + "y40.1"],
+                "f", end,
                 lambda: [move(4, 6, 1, RIGHT), move(4, 5, 1, LEFT), move(4, 7, 1, ACROSS)], 0.1
             )
-            last = [name + "f.%d" % i for i in range(3)] + [name + "y40.0", name + "y40.1"]
+            last = [name + "f.%d" % i for i in range(3)] + end
         else:
             last = [name + "y4%d.0" % d for d in range(4)]
-        self.need[0] = line[1] + line[2] + line[3] + last
-        self.share()
+        self.need[0] = (line[1] + line[2] + line[3], last)
+        self.share(True)
 
 
 class RouteB(Route):
@@ -104,10 +134,19 @@
             return [move(src, 8 * p + 1, 1, (0, p, 0)), move(src, 8 * p, 1, (0, -p, 0))]
 
         got = {}
-        if mode == 0:
+        if mode >= 3:
+            self.task("y4", ready, lambda: [move(0, 1, 1, (0, 4, 0))], 0.15)
+            got[4] = [name + "y4.0"]
+        if mode == 4:
+            self.task("y2", ready, lambda: to(2), 0.01)
+            self.task("y1", ready, lambda: to(1), 0.02)
+            got[1], got[2] = [name + "y1.0", name + "y1.1"], [name + "y2.0", name + "y2.1"]
+            self.task("y3", got[2], lambda: [move(17, 25, 1, UP), move(16, 24, 1, DOWN)])
+            got[3] = [name + "y3.0", name + "y3.1"]
+        elif mode in (0, 3):
             self.task("y1", ready, lambda: to(1))
             got[1] = [name + "y1.0", name + "y1.1"]
-            for p in (1, 2, 3):
+            for p in (1, 2) if mode else (1, 2, 3):
                 if p < 3:
                     def work(g=8 * p):
                         return [move(g + 1, g + 9, 1, UP), move(g, g + 8, 1, DOWN)]
@@ -151,7 +190,7 @@
             self.task("r%d" % p, near, relay, 0.05)
             mine = (got[p] if p else []) + near + ["%sr%d.%d" % (name, p, i) for i in (0, 1)]
             self.need[p % 4] = self.need.get(p % 4, []) + mine
-        self.share()
+        self.share(False)
 
 
 def routes(post, send, bufs, ready):
@@ -166,12 +205,11 @@
 
 def work_plan(post, send, bufs, act, nz):
     keys, vals, ques, grads = routes(post, send, bufs, ((), (), (), ()))
-    w_in = []
+    others = far_first(nz)
     if nz > 1:
         post("W", ["Ky20.0"], act("W", 0), 0.9)
-        for dz in range(1, nz):
-            post("w%d" % dz, ["scol", "W.%d" % (dz - 1)], act("w", dz), 9.5)
-            w_in += ["W.%d" % (dz - 1), "w%d.0" % dz]
+    for i, dz in enumerate(others):
+        post("w%d" % dz, ["col1", "dq", "W.%d" % i], act("w", dz), 11.5)
     for p in WAVES:
         post("score%d" % p, keys[p], act("score", p), 10)
         post("pv%d" % p, vals[p] + ["score%d" % p], act("pv", p), 10.5)
@@ -179,15 +217,17 @@
     post("stat", ["pv%d" % p for p in WAVES], act("stat", 0), 5)
     line = ["stat.%d" % i for i in range(7)]
     post("scol", line, act("scol", 0), 0)
-    col = line + ["scol.%d" % i for i in range(NY - 1)]
     for p in WAVES:
         post("slope%d" % p, ["stat"], act("slope", p), 14)
-        post("col%d" % p, col + ["pre%d" % p], act("col", p), 12)
+        post("col%d" % p, line + (["scol.%d" % (2 * p - 2), "scol.%d" % (2 * p - 1)] if p else ["scol.6"]) + ["pre%d" % p], act("col", p), 12)
     post("dq", ["slope%d" % p for p in WAVES], act("dq", 0), 15)
     post("dkv", ["col%d" % p for p in WAVES], act("dkv", 0), 11)
     if nz > 1:
         post("att", ["stat"], act("att", 0), 5.5)
-    post("out", ["stat"] + w_in + ["att.%d" % i for i in range(nz - 1)], act("out", 0), 20)
+    post("out0", ["stat"], act("out", 0), 16)
+    for i, dz in enumerate(others):
+        post("out%d" % dz, ["out0", "W.%d" % i, "w%d.0" % dz, "att.%d" % i], act("out", dz), 20)
+    post("put", ["out%d" % dz for dz in [0] + others], act("put", 0), 21)
 
 
 def nt(left, right):
@@ -217,7 +257,7 @@
         pl.semaphore_signal(sem, inc=1, device_id=who, device_id_type=MESH)
 
     barrier = pltpu.get_barrier_semaphore()
-    chips = [(dx, 0) for dx in DX[1:]] + [(0, dy) for dy in range(1, NY)]
+    chips = [(dx, 0) for dx in DX[1:]] + [(0, dy) for dy in NEAR]
     for dx, dy in chips:
         signal(barrier, at(dx, dy, c))
 
@@ -318,9 +358,12 @@
 
     def spread(_):
         out = []
-        for d in (4, 3, 5, 2, 6, 1, 7):
-            slot = 1 if d == 4 else (2 * d + 1 if d < 4 else 2 * (NY - d))
-            out.append(push(stat.at[pl.ds(0, 8)], stat.at[pl.ds(8 * slot, 8)], at(dy=d)))
+        for p in WAVES:
+            if p:
+                out.append(push(stat.at[pl.ds(0, 8)], stat.at[pl.ds(16 * p + 8, 8)], at(dy=p)))
+                out.append(push(stat.at[pl.ds(0, 8)], stat.at[pl.ds(16 * p, 8)], at(dy=-p)))
+            else:
+                out.append(push(stat.at[pl.ds(0, 8)], stat.at[pl.ds(8, 8)], at(dy=4)))
         return out
 
     def slope(p):
@@ -343,7 +386,7 @@
     def col(p):
         probs, slopes = [], []
         for i, (core, k, dxi) in enumerate(cells(p)):
-            st = stat[(2 * p + k) * 8 + core * 4 + dxi]
+            st = stat[16 * p + 8 * k + 4 * core + dxi]
             e = jnp.exp2(s_scr[p * 16 + i] - st[0:1])
             probs.append(e.astype(BF))
             slopes.append((e * (d_scr[p * 16 + i] - st[1:2])).astype(BF))
@@ -368,7 +411,7 @@
         def _():
             pl.semaphore_wait(go_sem, 1)
 
-        for dz in range(1, nz):
+        for dz in far_first(nz):
             first = pl.multiple_of(((z + nz - dz) % nz) * ow + c * half, 16)
             out.append(push(w_own.at[pl.ds(first, half)], w_all.at[dz, part], at(dz=-dz)))
         return out
@@ -377,17 +420,20 @@
         return [push(w_all.at[dz, part], w_all.at[dz, part], at(core=1))]
 
     def heads(_):
-        return [push(att.at[0], att.at[dz], at(dz=-dz)) for dz in range(1, nz)]
-
-    def project(_):
-        out = nt(val["att"], w_own[pl.ds(pl.multiple_of(z * ow, 16), ow)])
-        for dz in range(1, nz):
-            out = out + nt(att[dz], w_all[dz])
-        out_ref[...] = out.astype(BF)
+        return [push(att.at[0], att.at[dz], at(dz=-dz)) for dz in far_first(nz)]
+
+    def project(dz):
+        if dz:
+            val["out"] = val["out"] + nt(att[dz], w_all[dz])
+        else:
+            val["out"] = nt(val["att"], w_own[pl.ds(pl.multiple_of(z * ow, 16), ow)])
+
+    def put_out(_):
+        out_ref[...] = val["out"].astype(BF)
 
     acts = {
         "score": score, "pv": pv, "pre": pre, "stat": finish, "scol": spread, "slope": slope, "col": col, "dq": put_dq,
-        "dkv": put_dkv, "W": weights, "w": weight, "att": heads, "out": project,
+        "dkv": put_dkv, "W": weights, "w": weight, "att": heads, "out": project, "put": put_out,
     }
     tasks = {}
 
@@ -395,7 +441,7 @@
         tasks[name] = (waits, work)
 
     work_plan(post, send, (ka, vb, qa, ob), lambda kind, i: functools.partial(acts[kind], i), nz)
-    names = [n for n in " ".join(ORDER).split() if n in tasks]
+    names = [list(tasks)[i] for i in ORDER]
     assert sorted(names) == sorted(tasks)
     coming = {}
     for name in names:

time: 56.2 us -> 54.6 us (0.972)
  Pallas kernels: 55.3 us -> 53.6 us
    pallas_call x1, Pallas kernels: 53.6 us -> 52 us  [local(): pl.pallas_call(functools.partial(kernel, nz, ow), out_shape=shapes, in_sp...]
where the time goes in v3:
time: 54.6 us; the launch traced here: 54.3 us
  Pallas kernels  53.6 us (98%)
  between operations  0.64 us (1%)
    pallas_call x1, Pallas kernels, local(): pl.pallas_call(functools.partial(kernel, nz, ow), out_shape=shapes, in_sp...  52 us
    pallas_call x1, Pallas kernels, local(): pl.pallas_call(hand_over, out_shape=shapes, in_specs=[vmem] * 4, out_spec...  1.64 us

profile of v3, /device:TPU:1, one launch (start us, length us, event | category | flops | bytes accessed | tf_op | source)
XLA Modules:
  0.0 54.3 jit_solution(337265625802717837)
XLA Ops:
  0.6 52.0 %shard_map.102 = (bf16[128,640]{1,0:T(8,128)(2,1)}, bf16[128,128]{1,0:T(8,128)(2,1)}, bf16[128,128]{1,0:T(8,128)(2,1)}, bf16[128,128]{1,0:T(8,128)(2,1)}) custom-call(bf16[128,128]{1,0:T(8,128)(2,1)} %q_hbm.1, bf16[128,128]{1,0:T(8,128)(2,1)} %k_hbm.1, bf16[128,128]{1,0:T(8,128)(2,1)} %v_hbm.1, bf16[5120,128]{1,0:T(8,128)(2,1)} %w_hbm.1, ...), custom_call_target="tpu_custom_call" | custom-call | tf_op jit(solution)/shard_map/pallas_call | solution.py:477
  52.7 1.6 %shard_map.103 = (bf16[128,640]{1,0:T(8,128)(2,1)}, bf16[128,128]{1,0:T(8,128)(2,1)}, bf16[128,128]{1,0:T(8,128)(2,1)}, bf16[128,128]{1,0:T(8,128)(2,1)}) custom-call(bf16[128,640]{1,0:T(8,128)(2,1)} %get-tuple-element.8.refs_0_, bf16[128,128]{1,0:T(8,128)(2,1)} %get-tuple-element.9.refs_1_, bf16[128,128]{1,0:T(8,128)(2,1)} %get-tuple-element.10.refs_2_, ...), custom_call_target="tpu_custom_call" | custom-call | tf_op jit(solution)/shard_map/pallas_call | solution.py:498
